TPU v7x, 32 devices: a whole 2x2x4 slice. The times are simulated.
32 devices in a mesh: outer: 4 (over z), inner: 8 (over y, x, core).
Axes of the slice: x: 2, y: 2, z: 4, core: 2. Of those that a mesh axis runs over, the one named last changes fastest.
Arguments:
- patches: bfloat16 [128, 128, 1024], P(('outer', 'inner')), may hold values from -6 to 6
- cotangent: bfloat16 [128, 128, 1024], P(('outer', 'inner')), may hold values from -0.28125 to 0.28125
- segment_ids: int32 [128, 128], P(('outer', 'inner')), may hold values from 0 to 7, never falling along the last dimension, each value on 1 to 64 neighbouring positions
- live_packs: int32 [32], P(('outer', 'inner')), may hold values from 1 to 4, as said below
- norm_gain: float32 [1024], replicated, may hold values from 0.25 to 1.75
- qkv_weight: bfloat16 [1024, 3072], P('inner'), may hold values from -0.1875 to 0.1875
- out_weight: bfloat16 [1024, 1024], P('inner'), may hold values from -0.1875 to 0.1875
- signs_qkv: int32 [3072], replicated, may hold values from 0 to 1
- signs_out: int32 [1024], replicated, may hold values from 0 to 1
Outputs:
- qkv_grad: float32 [1024, 3072], P('inner')
- out_grad: float32 [1024, 1024], P('inner')
- gain_grad: float32 [1024], replicated
Inputs may be any that keep to these rules, and one draw needn't show every extreme that they name: `live_packs`: the live slots of a device are its first ones; in every draw some device has all 4 slots live.
All inputs are finite; a program needn't handle non-finite values.
Results may differ from a plain program's by a relative error of at most 0.03.
Values may be sent and summed in bfloat16 or wider, within the bound.
A program may use at most 64 MiB of HBM per device.

v0:
```python
import jax
import jax.numpy as jnp
from jax import lax
from jax.sharding import PartitionSpec as P

HEAD_DIM = 64


EPSILON = 1e-06
CLIP_RATIO = 2.0
BLOCK_WIDTH = 128
BLOCK_SCALE = 0.08838834764831845


def hadamard_table():
    indices = jnp.arange(BLOCK_WIDTH, dtype=jnp.int32)
    common = jnp.zeros((BLOCK_WIDTH, BLOCK_WIDTH), jnp.int32)
    for level in range(7):
        stride = 2**level
        common = common + indices[:, None] // stride % 2 * (indices[None, :] // stride % 2)
    return (1 - 2 * (common % 2)).astype(jnp.float32) * BLOCK_SCALE


def normalize(inputs, norm_gain):
    center = inputs - jnp.mean(inputs, axis=-1, keepdims=True)
    spread = jnp.mean(center * center, axis=-1, keepdims=True)
    return center * lax.rsqrt(spread + EPSILON) * norm_gain


def attend(projected, segment_ids):
    pack_count, pack_length, triple_width = projected.shape
    model_width = triple_width // 3
    head_count = model_width // HEAD_DIM
    split = projected.astype(jnp.float32).reshape(pack_count, pack_length, 3, head_count, HEAD_DIM)
    queries = split[:, :, 0]
    keys_all = split[:, :, 1]
    values_all = split[:, :, 2]
    scores = jnp.einsum("bqhd,bkhd->bhqk", queries, keys_all) * HEAD_DIM ** (-0.5)
    allowed = segment_ids[:, :, None] == segment_ids[:, None, :]
    scores = jnp.where(allowed[:, None], scores, -1e30)
    top_score = lax.stop_gradient(jnp.max(scores, axis=-1, keepdims=True))
    exponent = jnp.exp(scores - top_score)
    probable = (exponent / jnp.sum(exponent, axis=-1, keepdims=True)).astype(jnp.bfloat16)
    mixed_heads = jnp.einsum("bhqk,bkhd->bqhd", probable.astype(jnp.float32), values_all)
    return mixed_heads.reshape(pack_count, pack_length, model_width).astype(jnp.bfloat16)


def contract_rows(left_side, right_side):
    return lax.dot_general(
        left_side, right_side, (((0,), (0,)), ((), ())), preferred_element_type=jnp.float32
    )


def contract_cols(left_side, right_side):
    return lax.dot_general(
        left_side, right_side, (((1,), (1,)), ((), ())), preferred_element_type=jnp.float32
    )


def layer_backward(patches, cotangent, segment_ids, norm_gain, qkv_weight, out_weight):
    pack_count, pack_length, model_width = patches.shape
    inputs = patches.astype(jnp.float32)
    normed, norm_pullback = jax.vjp(normalize, inputs, norm_gain)
    flat_hidden = normed.astype(jnp.bfloat16).reshape(-1, model_width)
    projected = jnp.dot(flat_hidden, qkv_weight, preferred_element_type=jnp.float32).astype(
        jnp.bfloat16
    )
    projected = projected.reshape(pack_count, pack_length, 3 * model_width)

    def attend_pack(stacked):
        return attend(stacked, segment_ids)

    attended, attend_pullback = jax.vjp(attend_pack, projected)
    flat_cotangent = cotangent.reshape(-1, model_width)
    grad_attended = contract_cols(flat_cotangent, out_weight).astype(jnp.bfloat16)
    grad_projected = attend_pullback(grad_attended.reshape(attended.shape))[0]
    flat_grad = grad_projected.reshape(-1, 3 * model_width)
    grad_hidden = contract_cols(flat_grad, qkv_weight)
    gain_term = norm_pullback(grad_hidden.reshape(normed.shape))[1]
    return (flat_hidden, flat_grad, attended.reshape(-1, model_width), gain_term)


def sign_values(sign_bits):
    return (1 - 2 * sign_bits).astype(jnp.float32)


def rotate(matrix, sign_bits):
    signed = matrix * sign_values(sign_bits)
    blocks = signed.reshape(-1, BLOCK_WIDTH)
    return jnp.dot(blocks, hadamard_table(), precision=lax.Precision.HIGHEST).reshape(matrix.shape)


def clip_blocks(rotated):
    blocks = rotated.reshape(-1, BLOCK_WIDTH)
    clip_bound = CLIP_RATIO * jnp.sqrt(jnp.mean(blocks * blocks, axis=-1, keepdims=True) + EPSILON)
    return jnp.clip(blocks, -clip_bound, clip_bound).reshape(rotated.shape)


def decode(summed, sign_bits):
    blocks = summed.reshape(-1, BLOCK_WIDTH)
    turned = jnp.dot(blocks, hadamard_table(), precision=lax.Precision.HIGHEST).reshape(
        summed.shape
    )
    return turned * sign_values(sign_bits)


def on_device(
    patches,
    cotangent,
    segment_ids,
    live_packs,
    norm_gain,
    qkv_weight,
    out_weight,
    signs_qkv,
    signs_out,
):
    whole_qkv, whole_out = (
        lax.all_gather(qkv_weight, "inner", axis=0, tiled=True),
        lax.all_gather(out_weight, "inner", axis=0, tiled=True),
    )
    slot_count, pack_length, model_width = patches.shape
    own_live = live_packs[0]
    all_patches, all_cotangent, all_segments = (patches, cotangent, segment_ids)
    first_pack = jnp.int32(0)
    total_slots = all_patches.shape[0]
    total_rows = total_slots * pack_length
    initial = (
        jnp.zeros((total_rows, model_width), jnp.bfloat16),
        jnp.zeros((total_rows, 3 * model_width), jnp.bfloat16),
        jnp.zeros((total_rows, model_width), jnp.bfloat16),
        jnp.zeros((model_width,), jnp.float32),
    )

    def visit_pack(position, running):
        hidden_rows, grad_rows, attended_rows, gain_total = running
        slot_index = jnp.where(position < own_live, position, slot_count + position - own_live)
        pack_inputs = lax.dynamic_slice_in_dim(all_patches, slot_index, 1, 0)
        pack_cotangent = lax.dynamic_slice_in_dim(all_cotangent, slot_index, 1, 0)
        pack_segments = lax.dynamic_slice_in_dim(all_segments, slot_index, 1, 0)
        hidden, grad_projected, attended, gain_term = layer_backward(
            pack_inputs, pack_cotangent, pack_segments, norm_gain, whole_qkv, whole_out
        )
        first_row = slot_index * pack_length
        return (
            lax.dynamic_update_slice_in_dim(hidden_rows, hidden, first_row, 0),
            lax.dynamic_update_slice_in_dim(grad_rows, grad_projected, first_row, 0),
            lax.dynamic_update_slice_in_dim(attended_rows, attended, first_row, 0),
            gain_total + gain_term,
        )

    hidden_rows, grad_rows, attended_rows, gain_total = lax.fori_loop(
        first_pack, own_live, visit_pack, initial
    )
    flat_cotangent = all_cotangent.reshape(-1, model_width)
    joined = lax.psum_scatter(
        jnp.concatenate(
            [contract_rows(hidden_rows, grad_rows), contract_rows(attended_rows, flat_cotangent)], 1
        ).astype(jnp.bfloat16),
        "inner",
        scatter_dimension=0,
        tiled=True,
    ).astype(jnp.float32)
    part_qkv = joined[:, : 3 * model_width]
    part_out = joined[:, 3 * model_width :]
    clipped_qkv = clip_blocks(rotate(part_qkv, signs_qkv))
    clipped_out = clip_blocks(rotate(part_out, signs_out))
    share_qkv, share_out = (
        lax.psum_scatter(
            clipped_qkv.astype(jnp.bfloat16), "outer", scatter_dimension=0, tiled=True
        ).astype(jnp.float32),
        lax.psum_scatter(
            clipped_out.astype(jnp.bfloat16), "outer", scatter_dimension=0, tiled=True
        ).astype(jnp.float32),
    )
    qkv_grad, out_grad = (
        lax.all_gather(
            decode(share_qkv, signs_qkv).astype(jnp.bfloat16), "outer", axis=0, tiled=True
        ).astype(jnp.float32),
        lax.all_gather(
            decode(share_out, signs_out).astype(jnp.bfloat16), "outer", axis=0, tiled=True
        ).astype(jnp.float32),
    )
    gain_grad = lax.psum(gain_total, ("outer", "inner"))
    return (qkv_grad, out_grad, gain_grad)


def solution(mesh):
    return jax.shard_map(
        on_device,
        mesh=mesh,
        in_specs=(
            P(("outer", "inner"), None, None),
            P(("outer", "inner"), None, None),
            P(("outer", "inner"), None),
            P(("outer", "inner")),
            P(),
            P("inner", None),
            P("inner", None),
            P(),
            P(),
        ),
        out_specs=(P("inner", None), P("inner", None), P()),
        check_vma=False,
    )
```

profile of v0, /device:TPU:1, one launch (start us, length us, event | category | flops | bytes accessed | tf_op | source)
XLA Modules:
  0.0 368.9 jit_solution(8739820856820663604)
XLA Ops:
  8.7 31.6 %all-gather.3.cloned.1.call-done = bf16[1024,1024]{1,0:T(8,128)(2,1)} async-done(((bf16[128,1024]{1,0:T(8,128)(2,1)}), bf16[1024,1024]{1,0:T(8,128)(2,1)}) %all-gather.3.cloned.1.call-update) | async-done | bytes 2097168 | tf_op jit(solution)/shard_map/all_gather | solution.py:120
  40.3 47.4 %all-gather.5.cloned.1.call-done = bf16[1024,3072]{1,0:T(8,128)(2,1)} async-done(((bf16[128,3072]{1,0:T(8,128)(2,1)}), bf16[1024,3072]{1,0:T(8,128)(2,1)}) %all-gather.5.cloned.1.call-update) | async-done | bytes 6291472 | tf_op jit(solution)/shard_map/all_gather | solution.py:119
  89.9 1.9 broadcast_in_dim.43
  91.8 52.3 %while.16 = (s32[]{:T(128)}, bf16[512,1024]{1,0:T(8,128)(2,1)}, bf16[512,3072]{0,1:T(8,128)(2,1)}, bf16[512,1024]{0,1:T(8,128)(2,1)}, f32[1024]{0:T(1024)S(1)}, ...) while((s32[]{:T(128)}, bf16[512,1024]{1,0:T(8,128)(2,1)}, ...), condition=%wide.region_7.8_spmd, body=%wide.region_0.7_spmd.sunk | while | flops 2091536640 | bytes 58925460 | solution.py:152
  96.8 1.8 convolution_convert_fusion.10
  98.8 4.0 %convolution_convert_fusion.9 = bf16[128,3072]{1,0:T(8,128)(2,1)S(1)} fusion(bf16[1024,3072]{1,0:T(8,128)(2,1)} %get-tuple-element.270, f32[1024]{0:T(1024)S(1)} %get-tuple-element.266, f32[128]{0:T(128)S(1)} %add_rsqrt_fusion.2, f32[128]{0:T(128)S(1)} %broadcast_multiply_fusion.2, bf16[4,128,1024]{2,1,0:T(8,128)(2,1)} %get-tuple-element.265, ...), kind=kOutput, calls=%fused_computation.1.clone.1 | convolution fusion | flops 806354944 | bytes 7345156 | tf_op jit(solution)/shard_map/while/body/dot_general | solution.py:65
  103.9 1.9 constant_dynamic-update-slice_fusion.6
  105.8 1.5 fusion.108
  107.4 1.3 convolution_convert_fusion.11
  112.6 3.2 fusion.110
  122.6 1.8 convolution_convert_fusion.10
  124.6 4.0 %convolution_convert_fusion.9 = bf16[128,3072]{1,0:T(8,128)(2,1)S(1)} fusion(bf16[1024,3072]{1,0:T(8,128)(2,1)} %get-tuple-element.270, f32[1024]{0:T(1024)S(1)} %get-tuple-element.266, f32[128]{0:T(128)S(1)} %add_rsqrt_fusion.2, f32[128]{0:T(128)S(1)} %broadcast_multiply_fusion.2, bf16[4,128,1024]{2,1,0:T(8,128)(2,1)} %get-tuple-element.265, ...), kind=kOutput, calls=%fused_computation.1.clone.1 | convolution fusion | flops 806354944 | bytes 7345156 | tf_op jit(solution)/shard_map/while/body/dot_general | solution.py:65
  129.7 1.9 constant_dynamic-update-slice_fusion.6
  131.6 1.5 fusion.108
  138.4 3.2 fusion.110
  144.1 2.9 convolution_convert_fusion.5
  147.1 5.5 %convolution_convert_fusion.4 = bf16[1024,3072]{1,0:T(8,128)(2,1)} fusion(bf16[512,1024]{1,0:T(8,128)(2,1)S(1)} %copy-done.4, bf16[512,3072]{0,1:T(8,128)(2,1)S(1)} %copy-done.2), kind=kOutput, calls=%fused_computation.52 | convolution fusion | flops 3224371200 | bytes 10485760 | tf_op jit(solution)/shard_map/dot_general | solution.py:49
  152.6 6.8 %pad_maximum_fusion = bf16[1024,4096]{1,0:T(8,128)(2,1)} fusion(bf16[1024,1024]{1,0:T(8,128)(2,1)S(1)} %convolution_convert_fusion.5, bf16[1024,3072]{1,0:T(8,128)(2,1)} %convolution_convert_fusion.4), kind=kLoop, calls=%fused_computation.51 | loop fusion | flops 16777216 | bytes 16777216 | tf_op jit(solution)/shard_map/concatenate | solution.py:157
  160.1 121.5 %reduce-scatter.4.cloned.1.call-done = bf16[128,4096]{1,0:T(8,128)(2,1)} async-done(((bf16[1024,4096]{1,0:T(8,128)(2,1)}), bf16[128,4096]{1,0:T(8,128)(2,1)}) %reduce-scatter.4.cloned.1.call-update) | async-done | bytes 1048592 | tf_op jit(solution)/shard_map/reduce_scatter | solution.py:156
  281.7 1.4 convert_element_type.101
  285.5 1.8 multiply_reduce_fusion
  290.9 40.0 %psum.7 = f32[1024]{0:T(1024)} all-reduce(f32[1024]{0:T(1024)S(1)} %get-tuple-element.72), channel_id=1, replica_groups=mesh['outer'=4,'inner'=8] {'outer','inner'}, use_global_device_ids=true, to_apply=%region_13.14 | all-reduce | flops 1024 | bytes 8192 | tf_op jit(solution)/shard_map/psum | solution.py:184
  332.2 11.0 %all_gather.15 = bf16[128,1024]{1,0:T(8,128)(2,1)S(1)} all-gather(bf16[32,1024]{1,0:T(8,128)(2,1)S(1)} %multiply_convert_fusion.1), channel_id=1, replica_groups=mesh['outer'=4,'inner'=8] {'outer'}, dimensions={0}, use_global_device_ids=true | all-gather | bytes 327680 | tf_op jit(solution)/shard_map/all_gather | solution.py:180
  345.7 15.3 %all_gather.14 = bf16[128,3072]{1,0:T(8,128)(2,1)S(1)} all-gather(bf16[32,3072]{1,0:T(8,128)(2,1)S(1)} %multiply_convert_fusion), channel_id=1, replica_groups=mesh['outer'=4,'inner'=8] {'outer'}, dimensions={0}, use_global_device_ids=true | all-gather | bytes 983040 | tf_op jit(solution)/shard_map/all_gather | solution.py:177
  (107 shorter events, 36.7 us)
Async XLA Ops:
  7.2 84.7 %copy-start.3 = (f32[1024]{0:T(1024)S(1)}, f32[1024]{0:T(1024)}, u32[]{:S(2)}) copy-start(f32[1024]{0:T(1024)} %param.15) | copy-start | bytes 12292
  7.2 33.2 %all-gather.3.cloned.1.call-start = ((), (), s32[]{:S(2)}) async-start(), calls=%async_computation.3 | async-start | bytes 2359296 | tf_op jit(solution)/shard_map/all_gather | solution.py:120
  7.9 79.9 %all-gather.5.cloned.1.call-start = ((), (), s32[]{:S(2)}) async-start(), calls=%async_computation.4 | async-start | bytes 7077888 | tf_op jit(solution)/shard_map/all_gather | solution.py:119
  8.7 273.0 %reduce-scatter.4.cloned.1.call-start = ((), (), s32[]{:S(2)}) async-start(), calls=%async_computation.5 | async-start | bytes 9437184 | tf_op jit(solution)/shard_map/reduce_scatter | solution.py:156
  40.3 51.5 %copy-start = (bf16[1024,1024]{1,0:T(8,128)(2,1)S(1)}, bf16[1024,1024]{1,0:T(8,128)(2,1)}, u32[]{:S(2)}) copy-start(bf16[1024,1024]{1,0:T(8,128)(2,1)} %all-gather.3.cloned.1.call-done) | copy-start | bytes 6291460
  107.4 1.8 copy-start.1
  109.6 2.2 slice-start
  110.1 2.5 slice-start.1
  133.2 1.8 copy-start.1
  135.4 2.2 slice-start
  135.9 2.5 slice-start.1
  144.1 3.0 copy-start.2
  144.1 3.0 copy-start.4
  159.4 0.7 copy-start.6
  159.4 0.7 copy-start.5
  159.4 171.5 %reduce-scatter.8.cloned.1.call-start = ((), (), s32[]{:S(2)}) async-start(), calls=%async_computation.7 | async-start | bytes 327680 | tf_op jit(solution)/shard_map/reduce_scatter | solution.py:172
  289.1 54.9 %reduce-scatter.6.cloned.1.call-start = ((), (), s32[]{:S(2)}) async-start(), calls=%async_computation.6 | async-start | bytes 983040 | tf_op jit(solution)/shard_map/reduce_scatter | solution.py:169
Sparse Core Ops, SparseCore 0:
  9.9 30.3 all-gather.2
  42.2 45.5 all-gather.4
  159.5 122.0 reduce-scatter.3
  289.2 17.9 reduce-scatter.7
  310.0 22.3 reduce-scatter.5
where the time goes:
time: 376 us; the launch traced here: 369 us
  waiting for transfers between devices  202 us (54%)
  blocking collectives  66.3 us (18%)
  matrix products  38.9 us (10%)
  local copies, waits for them, and re-layouts  22.1 us (6%)
  other arithmetic  20.3 us (5%)
  between operations  14 us (4%)
  loops' own time  4.81 us (1%)
    reduce_scatter x1, waiting for transfers between devices, on_device(): lax.psum_scatter(jnp.concatenate([contract_rows(hidden_rows, grad_rows),...  122 us
    all_gather x1, waiting for transfers between devices, on_device(): lax.all_gather(qkv_weight, 'inner', axis=0, tiled=True)  47.4 us
    psum x1, blocking collectives, on_device(): gain_grad = lax.psum(gain_total, ('outer', 'inner'))  40 us
    all_gather x1, waiting for transfers between devices, on_device(): lax.all_gather(out_weight, 'inner', axis=0, tiled=True)  31.6 us
    all_gather x1, blocking collectives, on_device(): lax.all_gather(decode(share_qkv, signs_qkv).astype(jnp.bfloat16), 'outer'...  15.3 us
    all_gather x1, blocking collectives, on_device(): lax.all_gather(decode(share_out, signs_out).astype(jnp.bfloat16), 'outer'...  11 us
    dot_general x4, matrix products, contract_cols(): lax.dot_general(left_side, right_side, (((1,), (1,)), ((), ())), preferre...  10 us
    dot_general x2, matrix products, contract_rows(): lax.dot_general(left_side, right_side, (((0,), (0,)), ((), ())), preferre...  8.43 us
  transfers between devices with their start and end apart: 5, of which 3 were waited for; matrix products, arithmetic and copies ran while one was open for 1% of the time, Pallas kernels for 0%

commit v1 on v0

v1 whole, which is shorter than its diff:
```python
import functools

import jax
import jax.numpy as jnp
from jax import lax
from jax.experimental import pallas as pl
from jax.experimental.pallas import tpu as pltpu
from jax.sharding import PartitionSpec as P

HEAD_DIM = 64
EPSILON = 1e-06
CLIP_RATIO = 2.0
BLOCK = 128
BLOCK_SCALE = 0.08838834764831845
GROUP = 256
F32 = jnp.float32
BF16 = jnp.bfloat16
MESH = pl.DeviceIdType.MESH


def dot_nn(a, b):
    return lax.dot_general(a, b, (((1,), (0,)), ((), ())), preferred_element_type=F32)


def dot_nt(a, b):
    return lax.dot_general(a, b, (((1,), (1,)), ((), ())), preferred_element_type=F32)


def dot_tn(a, b):
    return lax.dot_general(a, b, (((0,), (0,)), ((), ())), preferred_element_type=F32)


def hadamard():
    rows = lax.broadcasted_iota(jnp.int32, (BLOCK, BLOCK), 0)
    cols = lax.broadcasted_iota(jnp.int32, (BLOCK, BLOCK), 1)
    common = rows & cols
    total = jnp.zeros_like(common)
    for level in range(7):
        total = total + ((common >> level) & 1)
    return (1 - 2 * (total & 1)).astype(F32).astype(BF16)


def turn(block, table):
    high = block.astype(BF16)
    low = (block - high.astype(F32)).astype(BF16)
    return (dot_nn(high, table) + dot_nn(low, table)) * BLOCK_SCALE


class Plan:
    def __init__(self, n_outer, n_inner, packs, length, width, rows):
        self.no, self.n = n_outer, n_inner
        self.bits = n_inner.bit_length() - 1
        self.packs, self.length, self.width, self.rows = packs, length, width, rows
        self.total = packs * length
        self.groups = width // GROUP
        self.share = rows // n_outer
        self.wire = BF16 if self.share % 16 == 0 else F32
        self.chunks = self.groups + 1
        self.cols = [3 * GROUP] * self.groups + [width]
        upper = list(range(self.bits - 1))
        self.orders = [upper[::-1], upper]
        per_gather = 2 * self.bits
        per_scatter = 1 + 2 * (self.bits - 1)
        per_outer = 2 * (self.no - 1)
        self.messages = (
            self.chunks * (per_gather + per_scatter + per_outer) + (self.no - 1) + self.bits
        )


def kernel(plan, x_ref, cot_ref, live_ref, bias_ref, gain_ref, wq_ref, wo_ref, sq_ref, so_ref,
           oq_ref, oo_ref, og_ref, *scratch):
    names = list(scratch)

    def take(count):
        got = names[:count]
        del names[:count]
        return got

    send_sem, recv_sem, hid, hid_t, cot, proj, gatt, att, att_t, gproj, gacc, gpart, gall = take(13)
    ch = plan.chunks
    weights, grads, from_twin, sums = take(ch), take(ch), take(ch), take(ch)
    clipped, from_outer, decoded = take(ch), take(ch), take(ch)
    steps = plan.bits - 1
    got_half = [[take(steps) for _ in range(2)] for _ in range(ch)]
    sum_half = [[take(steps - 1) for _ in range(2)] for _ in range(ch)]

    outer, inner = lax.axis_index("outer"), lax.axis_index("inner")
    bits, rows, length, no = plan.bits, plan.rows, plan.length, plan.no
    half = rows // 2
    stride = [2 ** (bits - 1 - b) for b in range(bits)]
    mine = [lax.rem(inner // stride[b], 2) for b in range(bits)]
    partner = [inner + (1 - 2 * mine[b]) * stride[b] for b in range(bits)]
    counter = [0]

    barrier = pltpu.get_barrier_semaphore()
    for b in range(bits):
        pl.semaphore_signal(barrier, inc=1, device_id={"inner": partner[b]}, device_id_type=MESH)
    for j in range(1, no):
        pl.semaphore_signal(
            barrier, inc=1, device_id={"outer": lax.rem(outer + j, no)}, device_id_type=MESH
        )

    def message(src, dst, where):
        at = counter[0]
        counter[0] += 1
        return pltpu.make_async_remote_copy(
            src_ref=src, dst_ref=dst, send_sem=send_sem.at[at], recv_sem=recv_sem.at[at],
            device_id=where, device_id_type=MESH,
        )

    started = []

    def launch(messages):
        for one in messages:
            one.start()
            started.append(one)

    def arrive(messages):
        for one in messages:
            one.wait_recv()

    gathers = []
    for k in range(ch):
        levels = []
        for s in range(bits):
            level = []
            for h in range(2):
                order = plan.orders[h] + [bits - 1]
                spot = tuple(
                    slice(None) if b in order[:s] else mine[b] for b in range(bits)
                ) + (pl.ds(h * half, half),)
                ref = weights[k].at[spot]
                level.append(message(ref, ref, {"inner": partner[order[s]]}))
            levels.append(level)
        gathers.append(levels)

    def gather(k, s):
        if s > 0:
            arrive(gathers[k][s - 1])
        launch(gathers[k][s])

    own = tuple(mine)
    out = plan.groups
    weights[out][own] = wo_ref[...]
    for g in range(plan.groups):
        for part in range(3):
            at = part * plan.width + g * GROUP
            weights[g][own + (slice(None), pl.ds(part * GROUP, GROUP))] = wq_ref[:, at:at + GROUP]
    pl.semaphore_wait(barrier, bits + no - 1)

    gather_order = [out] + list(range(plan.groups))
    gather(out, 0)
    gather(0, 0)
    gather(1, 0)

    def norm_pack(p):
        at = pl.ds(pl.multiple_of(p * length, length), length)
        inputs = x_ref[at, :].astype(F32)
        center = inputs - jnp.mean(inputs, axis=-1, keepdims=True)
        spread = jnp.mean(center * center, axis=-1, keepdims=True)
        value = center * lax.rsqrt(spread + EPSILON) * gain_ref[...]
        hid[at, :] = value.astype(BF16)
        hid_t[:, at] = value.T.astype(BF16)
        cot[at, :] = (cot_ref[at, :].astype(F32) * live_ref[p][0:1, 0:1]).astype(BF16)

    pl.loop(0, plan.packs // 2)(norm_pack)
    gather(out, 1)
    gather(0, 1)
    pl.loop(plan.packs // 2, plan.packs)(norm_pack)
    gather(2, 0)
    gather(out, 2)
    gather(1, 1)
    gather(0, 2)
    arrive(gathers[out][bits - 1]) if bits == 3 else None

    table = hadamard()

    pending = []
    if bits != 3:
        for k in (out, 0):
            for s in range(3, bits):
                pending.append((k, s))
    for k in range(1, plan.groups):
        for s in range(bits):
            if (k, s) not in ((1, 0), (1, 1), (2, 0)):
                pending.append((k, s))

    def gather_upto(k):
        while any(entry[0] == k for entry in pending):
            gather(*pending.pop(0))

    if bits != 3:
        gather_upto(out)
        gather_upto(0)
        arrive(gathers[out][bits - 1])

    taken = bits - (GROUP // rows).bit_length() + 1

    def grad_att(g):
        spot = tuple((g >> (taken - 1 - b)) & 1 for b in range(taken))
        block = weights[out][spot].reshape(GROUP, plan.width)
        gatt[:, g * GROUP:(g + 1) * GROUP] = dot_nt(cot[...], block).astype(BF16)

    for g in range(plan.groups):
        grad_att(g)

    def project(g):
        arrive(gathers[g][bits - 1])
        for part in range(3):
            cols = pl.ds(part * GROUP, GROUP)
            block = weights[g][(slice(None),) * (bits + 1) + (cols,)]
            proj[:, cols] = dot_nn(hid[...], block.reshape(plan.width, GROUP)).astype(BF16)

    lane = lax.broadcasted_iota(jnp.int32, (length, BLOCK), 1)
    first = lane < HEAD_DIM

    def stack(value):
        zero = jnp.zeros_like(value)
        return jnp.concatenate([jnp.where(first, value, zero), jnp.where(first, zero, value)], 0)

    def pick(value):
        return jnp.where(first, value[:length], value[length:])

    def attend(g):
        def one(p):
            at = pl.ds(pl.multiple_of(p * length, length), length)
            bias = bias_ref[p]
            bias = jnp.concatenate([bias, bias], 0)
            for j in range(GROUP // BLOCK):
                cols = [pl.ds(part * GROUP + j * BLOCK, BLOCK) for part in range(3)]
                query, key, value = (proj[at, c] for c in cols)
                spot = g * GROUP + j * BLOCK
                queries = stack(query)
                scores = dot_nt(queries, key) * (HEAD_DIM ** -0.5) + bias
                power = jnp.exp(scores - jnp.max(scores, axis=-1, keepdims=True))
                prob = power / jnp.sum(power, axis=-1, keepdims=True)
                rounded = prob.astype(BF16)
                att[at, pl.ds(j * BLOCK, BLOCK)] = pick(dot_nn(rounded, value)).astype(BF16)
                grads_out = stack(gatt[at, spot:spot + BLOCK])
                grad_prob = dot_nt(grads_out, value).astype(BF16).astype(F32)
                inside = jnp.sum(grad_prob * prob, axis=-1, keepdims=True)
                grad_score = (prob * (grad_prob - inside) * (HEAD_DIM ** -0.5)).astype(BF16)
                gproj[at, cols[0]] = pick(dot_nn(grad_score, key)).astype(BF16)
                gproj[at, cols[1]] = dot_tn(grad_score, queries).astype(BF16)
                gproj[at, cols[2]] = dot_tn(rounded, grads_out).astype(BF16)

        pl.loop(0, plan.packs)(one)
        att_t[g * GROUP:(g + 1) * GROUP, :] = att[...].T

    def block_spot(i):
        return tuple((i >> (bits - 1 - b)) & 1 for b in range(bits))

    def weight_grad(k, left, right):
        tall = max(rows, GROUP)
        per = tall // rows
        for i in range(0, plan.n, per):
            product = dot_nn(left[i * rows:i * rows + tall, :], right[...]).astype(BF16)
            for e in range(per):
                grads[k][block_spot(i + e)] = product[e * rows:(e + 1) * rows]

    last = bits - 1
    live = {}

    def add(a, b):
        return a.astype(F32) + b.astype(F32)

    def stage_twin(k):
        spot = (slice(None),) * last
        msg = message(grads[k].at[spot + (1 - mine[last],)], from_twin[k], {"inner": partner[last]})
        launch([msg])
        live[k] = [msg]

    def stage_half(k, s):
        arrive(live[k])
        messages = []
        if s == 0:
            sums[k][...] = add(
                grads[k][(slice(None),) * last + (mine[last],)], from_twin[k][...]
            ).astype(BF16)
        finals = []
        for h in range(2):
            order = plan.orders[h][::-1]
            if s == 0:
                source, remaining = sums[k], list(range(last))
                tail = (pl.ds(h * half, half),)
            else:
                remaining = [b for b in range(last) if b not in order[:s - 1]]
                before = sums[k] if s == 1 else sum_half[k][h][s - 2]
                tail = (pl.ds(h * half, half),) if s == 1 else ()
                spot = tuple(
                    mine[b] if b == order[s - 1] else slice(None) for b in remaining
                ) + tail
                value = add(before[spot], got_half[k][h][s - 1][...])
                remaining = [b for b in remaining if b != order[s - 1]]
                if s == steps:
                    finals.append(value)
                    continue
                sum_half[k][h][s - 1][...] = value.astype(BF16)
                source, tail = sum_half[k][h][s - 1], ()
            spot = tuple(
                1 - mine[b] if b == order[s] else slice(None) for b in remaining
            ) + tail
            messages.append(message(
                source.at[spot], got_half[k][h][s], {"inner": partner[order[s]]}
            ))
        if s < steps:
            launch(messages)
            live[k] = messages
            return
        stage_clip(k, finals)

    def signs_at(k, b):
        if k == out:
            at, ref = b * BLOCK, so_ref
        else:
            per = GROUP // BLOCK
            at, ref = (b // per) * plan.width + k * GROUP + (b % per) * BLOCK, sq_ref
        return at, (1 - 2 * ref[:, at:at + BLOCK]).astype(F32)

    def stage_clip(k, finals):
        whole = jnp.concatenate(finals, 0)
        partial = None
        for b in range(plan.cols[k] // BLOCK):
            block = whole[:, b * BLOCK:(b + 1) * BLOCK]
            at, signs = signs_at(k, b)
            if k != out:
                term = block * wq_ref[:, at:at + BLOCK].astype(F32)
                partial = term if partial is None else partial + term
            value = turn(block * signs, table)
            bound = CLIP_RATIO * jnp.sqrt(
                jnp.mean(value * value, axis=-1, keepdims=True) + EPSILON
            )
            value = jnp.clip(value, -bound, bound)
            clipped[k][:, :, b * BLOCK:(b + 1) * BLOCK] = value.reshape(
                no, plan.share, BLOCK
            ).astype(plan.wire)
        if k != out:
            gacc[...] = partial if k == 0 else gacc[...] + partial
        messages = []
        for j in range(1, no):
            there = lax.rem(outer + j, no)
            messages.append(message(
                clipped[k].at[there], from_outer[k].at[j - 1], {"outer": there}
            ))
        launch(messages)
        live[k] = messages

    def stage_decode(k):
        arrive(live[k])
        total = clipped[k][outer].astype(F32)
        for j in range(1, no):
            total = total + from_outer[k][j - 1].astype(F32)
        for b in range(plan.cols[k] // BLOCK):
            signs = signs_at(k, b)[1]
            value = turn(total[:, b * BLOCK:(b + 1) * BLOCK], table) * signs
            decoded[k][outer, :, b * BLOCK:(b + 1) * BLOCK] = value.astype(plan.wire)
        messages = []
        for j in range(1, no):
            ref = decoded[k].at[outer]
            messages.append(message(ref, ref, {"outer": lax.rem(outer + j, no)}))
        launch(messages)
        live[k] = messages

    def stage_store(k):
        arrive(live[k])
        for part in range(1 if k == out else 3):
            wide = plan.width if k == out else GROUP
            value = decoded[k][:, :, part * wide:(part + 1) * wide].astype(F32)
            value = value.reshape(rows, wide)
            if k == out:
                oo_ref[...] = value
            else:
                at = part * plan.width + k * GROUP
                oq_ref[:, at:at + GROUP] = value

    def stages(k):
        todo = [functools.partial(stage_half, k, s) for s in range(steps + 1)]
        return todo + [functools.partial(stage_decode, k), functools.partial(stage_store, k)]

    queues = []

    def advance():
        for queue in queues:
            if queue:
                queue.pop(0)()

    for g in range(plan.groups):
        gather_upto(g)
        project(g)
        if g + 1 < plan.groups:
            while pending and pending[0][0] <= g + 1:
                gather(*pending.pop(0))
        advance()
        attend(g)
        if pending:
            gather(*pending.pop(0))
        advance()
        weight_grad(g, hid_t, gproj)
        stage_twin(g)
        queues.append(stages(g))
        if pending:
            gather(*pending.pop(0))
        advance() if g > 0 else None

    weight_grad(out, att_t, cot)
    stage_twin(out)
    queues.append(stages(out))
    while len(queues[out - 1]) > 2:
        advance()

    ones = jnp.ones((8, BLOCK), F32)
    gpart[outer] = lax.dot_general(
        ones, gacc[...], (((1,), (1,)), ((), ())), precision=lax.Precision.HIGHEST,
        preferred_element_type=F32,
    )
    gain_messages = []
    for j in range(1, no):
        ref = gpart.at[outer]
        gain_messages.append(message(ref, ref, {"outer": lax.rem(outer + j, no)}))
    launch(gain_messages)
    advance()
    arrive(gain_messages)
    total = gpart[0]
    for j in range(1, no):
        total = total + gpart[j]
    gall[own] = total
    for b in range(bits):
        spot = tuple(slice(None) if e < b else mine[e] for e in range(bits))
        ref = gall.at[spot]
        step = message(ref, ref, {"inner": partner[b]})
        launch([step])
        if b < 2:
            advance()
        arrive([step])
    for i in range(plan.n):
        og_ref[i] = gall[block_spot(i)]
    while any(queues):
        advance()
    for one in started:
        one.wait_send()


def on_device(plan, patches, cotangent, segment_ids, live_packs, norm_gain, qkv_weight, out_weight,
              signs_qkv, signs_out):
    width, rows, no = plan.width, plan.rows, plan.no
    flat = (plan.total, width)
    live = (jnp.arange(plan.packs, dtype=jnp.int32) < live_packs[0]).astype(F32)
    live = jnp.broadcast_to(live[:, None, None], (plan.packs, 8, BLOCK))
    allowed = segment_ids[:, :, None] == segment_ids[:, None, :]
    bias = jnp.where(allowed, 0.0, -1e30).astype(F32)
    two = (2,) * plan.bits
    vmem = pltpu.VMEM
    scratch = [
        pltpu.SemaphoreType.DMA((plan.messages,)),
        pltpu.SemaphoreType.DMA((plan.messages,)),
        vmem(flat, BF16),
        vmem(flat[::-1], BF16),
        vmem(flat, BF16),
        vmem((plan.total, 3 * GROUP), BF16),
        vmem(flat, BF16),
        vmem((plan.total, GROUP), BF16),
        vmem(flat[::-1], BF16),
        vmem((plan.total, 3 * GROUP), BF16),
        vmem((rows, BLOCK), F32),
        vmem((no, 8, rows), F32),
        vmem(two + (8, rows), F32),
    ]
    for shape, kind in (
        (two + (rows,), BF16), (two + (rows,), BF16), (two[1:] + (rows,), BF16),
        (two[1:] + (rows,), BF16), ((no, plan.share), plan.wire),
        ((no - 1, plan.share), plan.wire), ((no, plan.share), plan.wire),
    ):
        scratch += [vmem(shape + (cols,), kind) for cols in plan.cols]
    steps = plan.bits - 1
    for count in (steps, steps - 1):
        for cols in plan.cols:
            for _ in range(2):
                for s in range(count):
                    scratch.append(vmem((2,) * (steps - 1 - s) + (rows // 2, cols), BF16))
    qkv_grad, out_grad, gain = pl.pallas_call(
        functools.partial(kernel, plan),
        out_shape=(
            jax.ShapeDtypeStruct((rows, 3 * width), F32),
            jax.ShapeDtypeStruct((rows, width), F32),
            jax.ShapeDtypeStruct((plan.n, 8, rows), F32),
        ),
        in_specs=[pl.BlockSpec(memory_space=pltpu.VMEM)] * 9,
        out_specs=[pl.BlockSpec(memory_space=pltpu.VMEM)] * 3,
        scratch_shapes=scratch,
        compiler_params=pltpu.CompilerParams(
            collective_id=0, has_side_effects=True, vmem_limit_bytes=58 * 2**20
        ),
    )(
        patches.reshape(flat), cotangent.reshape(flat), live, bias, norm_gain[None], qkv_weight,
        out_weight, signs_qkv[None], signs_out[None],
    )
    return qkv_grad, out_grad, gain[:, 0].reshape(width) / norm_gain


def solution(mesh):
    def device(patches, cotangent, segment_ids, live_packs, norm_gain, qkv_weight, *others):
        packs, length, width = patches.shape
        plan = Plan(
            mesh.shape["outer"], mesh.shape["inner"], packs, length, width, qkv_weight.shape[0]
        )
        return on_device(
            plan, patches, cotangent, segment_ids, live_packs, norm_gain, qkv_weight, *others
        )

    return jax.shard_map(
        device,
        mesh=mesh,
        in_specs=(
            P(("outer", "inner"), None, None),
            P(("outer", "inner"), None, None),
            P(("outer", "inner"), None),
            P(("outer", "inner")),
            P(),
            P("inner", None),
            P("inner", None),
            P(),
            P(),
        ),
        out_specs=(P("inner", None), P("inner", None), P()),
        check_vma=False,
    )
```

time: 376 us -> 136 us (0.36); the launches traced: 369 us -> 136 us
  waiting for transfers between devices: 202 us -> 0 us
  Pallas kernels: 0 us -> 128 us
  blocking collectives: 66.3 us -> 0 us
  matrix products: 38.9 us -> 0 us
  other arithmetic: 20.3 us -> 2.2 us
  local copies, waits for them, and re-layouts: 22.1 us -> 5 us
  between operations: 14 us -> 1.3 us
  loops' own time: 4.81 us -> 0 us
    pallas_call x0 -> x1, Pallas kernels: none -> 128 us  [on_device(): pl.pallas_call(functools.partial(kernel, plan), out_shape=(jax.ShapeDtype...]
    reduce_scatter x3 -> x0, waiting for transfers between devices: 122 us -> none  [the longest x1 122 us: on_device(): lax.psum_scatter(jnp.concatenate([contract_rows(hidden_rows, grad_rows),...]
    all_gather x2 -> x0, waiting for transfers between devices: 79.1 us -> none  [the longest x1 47.4 us: on_device(): lax.all_gather(qkv_weight, 'inner', axis=0, tiled=True)]
    psum x1 -> x0, blocking collectives: 40 us -> none  [on_device(): gain_grad = lax.psum(gain_total, ('outer', 'inner'))]
    dot_general x22 -> x0, matrix products: 35.8 us -> none  [the longest x4 10 us: contract_cols(): lax.dot_general(left_side, right_side, (((1,), (1,)), ((), ())), preferre...]
    all_gather x2 -> x0, blocking collectives: 26.3 us -> none  [the longest x1 15.3 us: on_device(): lax.all_gather(decode(share_qkv, signs_qkv).astype(jnp.bfloat16), 'outer'...]
    concatenate x1 -> x0, other arithmetic: 6.83 us -> none  [on_device(): jnp.concatenate([contract_rows(hidden_rows, grad_rows), contract_rows(att...]
    convert_element_type x8 -> x0, local copies, waits for them, and re-layouts: 5.27 us -> none  [the longest x2 2.35 us: layer_backward(): jnp.dot(flat_hidden, qkv_weight, preferred_element_type=jnp.float32)]
  transfers between devices with their start and end apart: 5 -> 0, of which waited for: 3 -> 0; matrix products, arithmetic and copies ran while one was open for 1% -> 0% of each run, Pallas kernels for 0% -> 0%
where the time goes in v1:
time: 136 us
  Pallas kernels  128 us (94%)
  local copies, waits for them, and re-layouts  5 us (4%)
  other arithmetic  2.2 us (2%)
    pallas_call x1, Pallas kernels, on_device(): pl.pallas_call(functools.partial(kernel, plan), out_shape=(jax.ShapeDtype...  128 us
    unnamed x6, local copies, waits for them, and re-layouts  3.56 us

profile of v1, /device:TPU:1, one launch (start us, length us, event | category | flops | bytes accessed | tf_op | source)
XLA Modules:
  0.0 136.2 jit_solution(12789678462035990563)
XLA Ops:
  1.3 0.7 broadcast_in_dim.25.live_ref
  2.0 1.6 %compare_select_fusion.bias_ref = f32[4,128,128]{2,1,0:T(8,128)} fusion(s32[4,128]{1,0:T(4,128)} %param.11), kind=kLoop, calls=%fused_computation | loop fusion | flops 131072 | bytes 264192 | tf_op jit(solution)/shard_map/jit(_where)/select_n | solution.py:450
  3.6 0.0 copy-start.1
  3.6 127.7 %shard_map.112 = (f32[128,3072]{1,0:T(8,128)}, f32[128,1024]{1,0:T(8,128)}, f32[8,8,128]{2,1,0:T(8,128)}) custom-call(bf16[512,1024]{1,0:T(8,128)(2,1)} %bitcast.8, bf16[512,1024]{1,0:T(8,128)(2,1)} %bitcast.9, f32[4,8,128]{2,1,0:T(8,128)} %broadcast_in_dim.25.live_ref, f32[4,128,128]{2,1,0:T(8,128)} %compare_select_fusion.bias_ref, f32[1,1024]{1,0:T(1,128)} %bitcast.10, ...), custom_call_target="tpu_custom_call" | custom-call | tf_op jit(solution)/shard_map/pallas_call | solution.py:480
  131.3 0.8 slice.3
  132.0 0.0 copy-done.1
  132.0 0.6 div.3
  132.6 0.0 copy-start
  132.7 2.8 %copy.15 = f32[128,3072]{1,0:T(8,128)} copy(f32[128,3072]{1,0:T(8,128)} %get-tuple-element.12) | data formatting | bytes 3145728
  135.4 0.0 copy-done
  135.4 0.8 copy.16
  (1 shorter events, 0.0 us)
Async XLA Ops:
  3.6 128.5 %copy-start.1 = (f32[1024]{0:T(1024)S(1)}, f32[1024]{0:T(1024)}, u32[]{:S(2)}) copy-start(f32[1024]{0:T(1024)} %param.13) | copy-start | bytes 12292
  132.6 2.8 %copy-start = (f32[128,1024]{1,0:T(8,128)S(1)}, f32[128,1024]{1,0:T(8,128)}, u32[]{:S(2)}) copy-start(f32[128,1024]{1,0:T(8,128)} %get-tuple-element.13) | copy-start | bytes 1572868

commit v2 on v1

--- a/solution.py
+++ b/solution.py
@@ -76,7 +76,7 @@
         del names[:count]
         return got
 
-    send_sem, recv_sem, hid, hid_t, cot, proj, gatt, att, att_t, gproj, gacc, gpart, gall = take(13)
+    send_sem, recv_sem, hid, hid_t, cot, proj, gatt, att_t, gproj, gacc, gpart, gall = take(12)
     ch = plan.chunks
     weights, grads, from_twin, sums = take(ch), take(ch), take(ch), take(ch)
     clipped, from_outer, decoded = take(ch), take(ch), take(ch)
@@ -218,34 +218,39 @@
         zero = jnp.zeros_like(value)
         return jnp.concatenate([jnp.where(first, value, zero), jnp.where(first, zero, value)], 0)
 
-    def pick(value):
-        return jnp.where(first, value[:length], value[length:])
+    paired = 2 if plan.packs % 2 == 0 else 1
 
     def attend(g):
-        def one(p):
+        def one(p, j):
             at = pl.ds(pl.multiple_of(p * length, length), length)
             bias = bias_ref[p]
-            bias = jnp.concatenate([bias, bias], 0)
-            for j in range(GROUP // BLOCK):
-                cols = [pl.ds(part * GROUP + j * BLOCK, BLOCK) for part in range(3)]
-                query, key, value = (proj[at, c] for c in cols)
-                spot = g * GROUP + j * BLOCK
-                queries = stack(query)
-                scores = dot_nt(queries, key) * (HEAD_DIM ** -0.5) + bias
-                power = jnp.exp(scores - jnp.max(scores, axis=-1, keepdims=True))
-                prob = power / jnp.sum(power, axis=-1, keepdims=True)
-                rounded = prob.astype(BF16)
-                att[at, pl.ds(j * BLOCK, BLOCK)] = pick(dot_nn(rounded, value)).astype(BF16)
-                grads_out = stack(gatt[at, spot:spot + BLOCK])
-                grad_prob = dot_nt(grads_out, value).astype(BF16).astype(F32)
-                inside = jnp.sum(grad_prob * prob, axis=-1, keepdims=True)
-                grad_score = (prob * (grad_prob - inside) * (HEAD_DIM ** -0.5)).astype(BF16)
-                gproj[at, cols[0]] = pick(dot_nn(grad_score, key)).astype(BF16)
-                gproj[at, cols[1]] = dot_tn(grad_score, queries).astype(BF16)
-                gproj[at, cols[2]] = dot_tn(rounded, grads_out).astype(BF16)
-
-        pl.loop(0, plan.packs)(one)
-        att_t[g * GROUP:(g + 1) * GROUP, :] = att[...].T
+            bias = jnp.concatenate([bias, bias], 1)
+            cols = [pl.ds(part * GROUP + j * BLOCK, BLOCK) for part in range(3)]
+            query, key, value = (proj[at, c] for c in cols)
+            spot = g * GROUP + j * BLOCK
+            queries = stack(query)
+            scores = dot_nt(key, queries) * (HEAD_DIM ** -0.5) + bias
+            power = jnp.exp(scores - jnp.max(scores, axis=0, keepdims=True))
+            prob = power * (1.0 / jnp.sum(power, axis=0, keepdims=True))
+            rounded = prob.astype(BF16)
+            mixed = dot_tn(value, rounded).astype(BF16)
+            att_t[spot:spot + HEAD_DIM, at] = mixed[:HEAD_DIM, :length]
+            att_t[spot + HEAD_DIM:spot + BLOCK, at] = mixed[HEAD_DIM:, length:]
+            grads_out = stack(gatt[at, spot:spot + BLOCK])
+            grad_prob = dot_nt(value, grads_out).astype(BF16).astype(F32)
+            inside = jnp.sum(grad_prob * prob, axis=0, keepdims=True)
+            grad_score = (prob * (grad_prob - inside) * (HEAD_DIM ** -0.5)).astype(BF16)
+            turned = dot_tn(key, grad_score)
+            turned = jnp.concatenate([turned[:HEAD_DIM, :length], turned[HEAD_DIM:, length:]], 0)
+            gproj[at, cols[0]] = turned.T.astype(BF16)
+            gproj[at, cols[1]] = dot_nn(grad_score, queries).astype(BF16)
+            gproj[at, cols[2]] = dot_nn(rounded, grads_out).astype(BF16)
+
+        @pl.loop(0, plan.packs // paired)
+        def _(step):
+            for e in range(paired):
+                for j in range(GROUP // BLOCK):
+                    one(step * paired + e, j)
 
     def block_spot(i):
         return tuple((i >> (bits - 1 - b)) & 1 for b in range(bits))
@@ -458,7 +463,6 @@
         vmem(flat, BF16),
         vmem((plan.total, 3 * GROUP), BF16),
         vmem(flat, BF16),
-        vmem((plan.total, GROUP), BF16),
         vmem(flat[::-1], BF16),
         vmem((plan.total, 3 * GROUP), BF16),
         vmem((rows, BLOCK), F32),

time: 136 us -> 131 us (0.963)
  Pallas kernels: 128 us -> 123 us
    pallas_call x1, Pallas kernels: 128 us -> 123 us  [on_device(): pl.pallas_call(functools.partial(kernel, plan), out_shape=(jax.ShapeDtype...]
where the time goes in v2:
time: 131 us
  Pallas kernels  123 us (94%)
  local copies, waits for them, and re-layouts  5 us (4%)
  other arithmetic  2.2 us (2%)
    pallas_call x1, Pallas kernels, on_device(): pl.pallas_call(functools.partial(kernel, plan), out_shape=(jax.ShapeDtype...  123 us
    unnamed x6, local copies, waits for them, and re-layouts  3.56 us

profile of v2, /device:TPU:1, one launch (start us, length us, event | category | flops | bytes accessed | tf_op | source)
XLA Modules:
  0.0 131.1 jit_solution(2307118595838389900)
XLA Ops:
  1.3 0.7 broadcast_in_dim.25.live_ref
  2.0 1.6 %compare_select_fusion.bias_ref = f32[4,128,128]{2,1,0:T(8,128)} fusion(s32[4,128]{1,0:T(4,128)} %param.11), kind=kLoop, calls=%fused_computation | loop fusion | flops 131072 | bytes 264192 | tf_op jit(solution)/shard_map/jit(_where)/select_n | solution.py:455
  3.6 0.0 copy-start.1
  3.6 122.6 %shard_map.112 = (f32[128,3072]{1,0:T(8,128)}, f32[128,1024]{1,0:T(8,128)}, f32[8,8,128]{2,1,0:T(8,128)}) custom-call(bf16[512,1024]{1,0:T(8,128)(2,1)} %bitcast.8, bf16[512,1024]{1,0:T(8,128)(2,1)} %bitcast.9, f32[4,8,128]{2,1,0:T(8,128)} %broadcast_in_dim.25.live_ref, f32[4,128,128]{2,1,0:T(8,128)} %compare_select_fusion.bias_ref, f32[1,1024]{1,0:T(1,128)} %bitcast.10, ...), custom_call_target="tpu_custom_call" | custom-call | tf_op jit(solution)/shard_map/pallas_call | solution.py:484
  126.2 0.8 slice.3
  127.0 0.0 copy-done.1
  127.0 0.6 div.3
  127.6 0.0 copy-start
  127.6 2.8 %copy.15 = f32[128,3072]{1,0:T(8,128)} copy(f32[128,3072]{1,0:T(8,128)} %get-tuple-element.12) | data formatting | bytes 3145728
  130.3 0.0 copy-done
  130.3 0.8 copy.16
  (1 shorter events, 0.0 us)
Async XLA Ops:
  3.6 123.4 %copy-start.1 = (f32[1024]{0:T(1024)S(1)}, f32[1024]{0:T(1024)}, u32[]{:S(2)}) copy-start(f32[1024]{0:T(1024)} %param.13) | copy-start | bytes 12292
  127.6 2.8 %copy-start = (f32[128,1024]{1,0:T(8,128)S(1)}, f32[128,1024]{1,0:T(8,128)}, u32[]{:S(2)}) copy-start(f32[128,1024]{1,0:T(8,128)} %get-tuple-element.13) | copy-start | bytes 1572868

commit v3 on v2

--- a/solution.py
+++ b/solution.py
@@ -167,7 +167,8 @@
     gather(out, 1)
     gather(0, 1)
     pl.loop(plan.packs // 2, plan.packs)(norm_pack)
-    gather(2, 0)
+    for k in range(2, plan.groups):
+        gather(k, 0)
     gather(out, 2)
     gather(1, 1)
     gather(0, 2)
@@ -182,7 +183,7 @@
                 pending.append((k, s))
     for k in range(1, plan.groups):
         for s in range(bits):
-            if (k, s) not in ((1, 0), (1, 1), (2, 0)):
+            if s > 0 and (k, s) != (1, 1):
                 pending.append((k, s))
 
     def gather_upto(k):
@@ -395,9 +396,11 @@
         if g + 1 < plan.groups:
             while pending and pending[0][0] <= g + 1:
                 gather(*pending.pop(0))
+        if pending:
+            gather(*pending.pop(0))
         advance()
         attend(g)
-        if pending:
+        for _ in range(min(2, len(pending))):
             gather(*pending.pop(0))
         advance()
         weight_grad(g, hid_t, gproj)

time: 131 us -> 133 us (1.015)
  Pallas kernels: 123 us -> 125 us
    pallas_call x1, Pallas kernels: 123 us -> 125 us  [on_device(): pl.pallas_call(functools.partial(kernel, plan), out_shape=(jax.ShapeDtype...]
where the time goes in v3:
time: 133 us
  Pallas kernels  125 us (94%)
  local copies, waits for them, and re-layouts  5 us (4%)
  other arithmetic  2.2 us (2%)
    pallas_call x1, Pallas kernels, on_device(): pl.pallas_call(functools.partial(kernel, plan), out_shape=(jax.ShapeDtype...  125 us
    unnamed x6, local copies, waits for them, and re-layouts  3.56 us

profile of v3, /device:TPU:1, one launch (start us, length us, event | category | flops | bytes accessed | tf_op | source)
XLA Modules:
  0.0 133.2 jit_solution(14024252017208752229)
XLA Ops:
  1.3 0.7 broadcast_in_dim.25.live_ref
  2.0 1.6 %compare_select_fusion.bias_ref = f32[4,128,128]{2,1,0:T(8,128)} fusion(s32[4,128]{1,0:T(4,128)} %param.11), kind=kLoop, calls=%fused_computation | loop fusion | flops 131072 | bytes 264192 | tf_op jit(solution)/shard_map/jit(_where)/select_n | solution.py:458
  3.6 0.0 copy-start.1
  3.6 124.7 %shard_map.112 = (f32[128,3072]{1,0:T(8,128)}, f32[128,1024]{1,0:T(8,128)}, f32[8,8,128]{2,1,0:T(8,128)}) custom-call(bf16[512,1024]{1,0:T(8,128)(2,1)} %bitcast.8, bf16[512,1024]{1,0:T(8,128)(2,1)} %bitcast.9, f32[4,8,128]{2,1,0:T(8,128)} %broadcast_in_dim.25.live_ref, f32[4,128,128]{2,1,0:T(8,128)} %compare_select_fusion.bias_ref, f32[1,1024]{1,0:T(1,128)} %bitcast.10, ...), custom_call_target="tpu_custom_call" | custom-call | tf_op jit(solution)/shard_map/pallas_call | solution.py:487
  128.2 0.8 slice.3
  129.0 0.0 copy-done.1
  129.0 0.6 div.3
  129.6 0.0 copy-start
  129.6 2.8 %copy.15 = f32[128,3072]{1,0:T(8,128)} copy(f32[128,3072]{1,0:T(8,128)} %get-tuple-element.12) | data formatting | bytes 3145728
  132.4 0.0 copy-done
  132.4 0.8 copy.16
  (1 shorter events, 0.0 us)
Async XLA Ops:
  3.6 125.4 %copy-start.1 = (f32[1024]{0:T(1024)S(1)}, f32[1024]{0:T(1024)}, u32[]{:S(2)}) copy-start(f32[1024]{0:T(1024)} %param.13) | copy-start | bytes 12292
  129.6 2.8 %copy-start = (f32[128,1024]{1,0:T(8,128)S(1)}, f32[128,1024]{1,0:T(8,128)}, u32[]{:S(2)}) copy-start(f32[128,1024]{1,0:T(8,128)} %get-tuple-element.13) | copy-start | bytes 1572868
